TPU v7x, 256 devices: a whole 4x4x8 slice. The times are simulated.
256 devices in a mesh: gx: 16 (over x_hi, z), gy: 16 (over y, x_lo, core).
Axes of the slice: x: 4 (x_hi: 2, x_lo: 2; x = x_hi * 2 + x_lo), y: 4, z: 8, core: 2. Of those that a mesh axis runs over, the one named last changes fastest.
Arguments:
- prediction: float32 [256, 256, 128], P('gx', 'gy'), may hold values from 0 to 1
- label_mask: int32 [256, 256, 128], P('gx', 'gy'), may hold values 0 or 1
- confidence: float32 [256, 256, 128], P('gx', 'gy'), may hold values from 0.5 to 1
Outputs:
- gradient: float32 [256, 256, 128], P('gx', 'gy')
- loss: float32 [], replicated
All inputs are finite; a program needn't handle non-finite values. No bound on the sum of `label_mask` on one device may be relied on, other than what follows from the above.
Results may differ from a plain program's by a relative error of at most 0.000025.
Values sent between devices are 32-bit elements; how exact they have to be, the bound alone decides.
No kernel may reach another device: no remote copies, remote signals or barrier semaphores. Data moves between devices by JAX's collectives and lax.ppermute only.
A program may use at most 128 MiB of HBM per device.

v0:
```python
import jax
import jax.numpy as jnp
from jax import lax
from jax.experimental import pallas as pl
from jax.experimental.pallas import tpu as pltpu
from jax.sharding import PartitionSpec as P

ITERS = 3
OWN = 16
WIDE = 10
NEAR = 5
YP = 40
Y0 = 12
XP = 40
HIGH, LOW = 36, 37
PLANE = XP * YP
LV = 32
DENSE = XP * LV
INF = float("inf")


def lanes():
    return lax.broadcasted_iota(jnp.int32, (8, 128), 1)


def sublanes():
    return lax.broadcasted_iota(jnp.int32, (8, 128), 0)


class Axes:
    def __init__(self, nb):
        size_x, size_y = lax.axis_size("gx"), lax.axis_size("gy")
        gx, gy = lax.axis_index("gx"), lax.axis_index("gy")
        self.first_x, self.last_x = gx == 0, gx == size_x - 1
        self.first_y, self.last_y = gy == 0, gy == size_y - 1
        self.nb = nb
        start = 0 if nb == 5 else 4
        self.low_s, self.low_b = divmod(Y0 - start, nb)
        self.up_s, self.up_b = divmod(Y0 + OWN - 1 - start, nb)
        sub, lane = sublanes(), lanes()
        self.low_y = (sub == self.low_s) & self.first_y
        self.up_y = (sub == self.up_s) & self.last_y
        self.low_z, self.up_z = lane == 0, lane == 127
        self.q_y = jnp.where(self.up_y, 0.25, 0.5)
        self.q_z = jnp.where(self.up_z, 0.25, 0.5)

    def rows(self, x, stand_in):
        below = jnp.where((x == WIDE) & self.first_x, stand_in, x - 1)
        above = jnp.where((x == WIDE + OWN - 1) & self.last_x, stand_in, x + 1)
        return below, above

    def q_x(self, x):
        return jnp.where((x == WIDE + OWN - 1) & self.last_x, 0.25, 0.5)

    def along_y(self, v, fill):
        nb = self.nb
        lower = [pltpu.roll(v[nb - 1], 1, 0)] + v[: nb - 1]
        upper = v[1:] + [pltpu.roll(v[0], 7, 0)]
        lower[self.low_b] = jnp.where(self.low_y, fill, lower[self.low_b])
        upper[self.up_b] = jnp.where(self.up_y, fill, upper[self.up_b])
        return lower, upper

    def along_z(self, v, fill):
        lower = [jnp.where(self.low_z, fill, pltpu.roll(a, 1, 1)) for a in v]
        upper = [jnp.where(self.up_z, fill, pltpu.roll(a, 127, 1)) for a in v]
        return lower, upper

    def back_y(self, gl, gu):
        nb = self.nb
        from_above = gl[1:] + [pltpu.roll(gl[0], 7, 0)]
        from_below = [pltpu.roll(gu[nb - 1], 1, 0)] + gu[: nb - 1]
        return [a + b for a, b in zip(from_above, from_below)]


def back_z(gl, gu):
    return [pltpu.roll(a, 127, 1) + pltpu.roll(b, 1, 1) for a, b in zip(gl, gu)]


def load(ref, base, x, nb):
    start = 0 if nb == 5 else 4
    return [ref[pl.ds(base + x * YP + start + b, 8, stride=nb), :] for b in range(nb)]


def store(ref, base, x, nb, v):
    start = 0 if nb == 5 else 4
    for b in range(nb):
        ref[pl.ds(base + x * YP + start + b, 8, stride=nb), :] = v[b]


def load_dense(ref, base, x):
    return [ref[pl.ds(pl.multiple_of(base + x * LV + 8 * b, 8), 8), :] for b in range(4)]


def store_dense(ref, base, x, v):
    for b in range(4):
        ref[pl.ds(pl.multiple_of(base + x * LV + 8 * b, 8), 8), :] = v[b]


def each(pick, *lists):
    out = lists[0]
    for other in lists[1:]:
        out = [pick(a, b) for a, b in zip(out, other)]
    return out


def pack_rows_kernel(pred, label, conf, target, send_a, send_b):
    even = lax.rem(lax.axis_index("gx"), 2) == 0
    target[...] = label[...].astype(jnp.float32) * conf[...]
    wide, near = WIDE * OWN, NEAR * OWN
    total = OWN * OWN
    for ref, last in ((send_a, even), (send_b, jnp.logical_not(even))):
        from_pred = pl.multiple_of(jnp.where(last, total - wide, 0), 8)
        from_target = pl.multiple_of(jnp.where(last, total - near, 0), 8)
        ref[0:wide, :] = pred[pl.ds(from_pred, wide), :]
        ref[wide : wide + near, :] = target[pl.ds(from_target, near), :]


XB, TB = 5, 4
SEND = (WIDE * XB + NEAR * TB) * 8


def pack_columns_kernel(pred, target, rows_a, rows_b, send_a, send_b, wide_pred, wide_target):
    even = lax.rem(lax.axis_index("gx"), 2) == 0
    wide, near, total = WIDE * OWN, NEAR * OWN, OWN * OWN
    wide_pred[wide : wide + total, :] = pred[...]
    wide_target[near : near + total, :] = target[...]
    for ref, after in ((rows_a, even), (rows_b, jnp.logical_not(even))):
        to_pred = pl.multiple_of(jnp.where(after, wide + total, 0), 8)
        to_target = pl.multiple_of(jnp.where(after, near + total, 0), 8)
        wide_pred[pl.ds(to_pred, wide), :] = ref[0:wide, :]
        wide_target[pl.ds(to_target, near), :] = ref[wide : wide + near, :]
    even = lax.rem(lax.axis_index("gy"), 2) == 0
    for ref, last in ((send_a, even), (send_b, jnp.logical_not(even))):
        start = jnp.where(last, OWN - WIDE, 0)
        for j in range(WIDE):
            for i in range(XB):
                ref[pl.ds((j * XB + i) * 8, 8), :] = wide_pred[pl.ds(i * 128 + start + j, 8, stride=OWN), :]
        start = jnp.where(last, OWN - NEAR, 0)
        for j in range(NEAR):
            for i in range(TB):
                ref[pl.ds((WIDE * XB + j * TB + i) * 8, 8), :] = wide_target[
                    pl.ds(i * 128 + start + j, 8, stride=OWN), :
                ]


def unpack(pred, target, rows_a, rows_b, cols_a, cols_b, vol, tvol):
    even = lax.rem(lax.axis_index("gx"), 2) == 0
    wide = WIDE * OWN

    def whole(i, _):
        own = pl.ds(pl.multiple_of(i * OWN, OWN), OWN)
        vol[pl.ds((WIDE + i) * YP + Y0, OWN), :] = pred[own, :]
        tvol[pl.ds((WIDE + i) * YP + Y0, OWN), :] = target[own, :]
        return 0

    lax.fori_loop(0, OWN, whole, 0)
    for ref, after in ((rows_a, even), (rows_b, jnp.logical_not(even))):
        to_pred = jnp.where(after, WIDE + OWN, 0)
        to_target = jnp.where(after, WIDE + OWN, WIDE - NEAR)

        def one(i, _, ref=ref, to_pred=to_pred):
            vol[pl.ds((to_pred + i) * YP + Y0, OWN), :] = ref[pl.ds(pl.multiple_of(i * OWN, OWN), OWN), :]
            return 0

        lax.fori_loop(0, WIDE, one, 0)

        def two(i, _, ref=ref, to_target=to_target):
            tvol[pl.ds((to_target + i) * YP + Y0, OWN), :] = ref[pl.ds(pl.multiple_of(wide + i * OWN, OWN), OWN), :]
            return 0

        lax.fori_loop(0, NEAR, two, 0)
    even = lax.rem(lax.axis_index("gy"), 2) == 0
    for ref, after in ((cols_a, even), (cols_b, jnp.logical_not(even))):
        y = jnp.where(after, Y0 + OWN, Y0 - WIDE)
        for j in range(WIDE):
            for i in range(XB):
                vol[pl.ds(i * 8 * YP + y + j, 8, stride=YP), :] = ref[pl.ds((j * XB + i) * 8, 8), :]
        y = jnp.where(after, Y0 + OWN, Y0 - NEAR)
        for j in range(NEAR):
            for i in range(TB):
                tvol[pl.ds((NEAR + i * 8) * YP + y + j, 8, stride=YP), :] = ref[
                    pl.ds((WIDE * XB + j * TB + i) * 8, 8), :
                ]
    for ref in (vol, tvol):
        for k in range(ITERS + 2):
            ref[pl.ds(k * PLANE + HIGH * YP, YP), :] = jnp.full((YP, 128), INF, jnp.float32)
            ref[pl.ds(k * PLANE + LOW * YP, YP), :] = jnp.full((YP, 128), -INF, jnp.float32)


def erode_rows(vol, k, first, last, axes):
    nb = axes.nb
    base = k * PLANE

    def row(x, _):
        below, above = axes.rows(x, HIGH)
        v = load(vol, base, x, nb)
        low, up = load(vol, base, below, nb), load(vol, base, above, nb)
        m = each(jnp.minimum, v, low, up, *axes.along_y(v, INF), *axes.along_z(v, INF))
        store(vol, base + PLANE, x, nb, m)
        return 0

    lax.fori_loop(first, last, row, 0)


def dilated(vol, base, x, axes):
    below, above = axes.rows(x, LOW)
    e = load(vol, base, x, 4)
    a = each(jnp.maximum, e, load(vol, base, below, 4), load(vol, base, above, 4))
    b = each(jnp.maximum, a, *axes.along_y(a, -INF))
    return each(jnp.maximum, b, *axes.along_z(b, -INF))


def skeleton_rows(vol, k, first, last, axes, skel, delta_ref):
    base = k * PLANE

    def row(x, _):
        d = dilated(vol, base + PLANE, x, axes)
        v = load(vol, base, x, 4)
        s = load_dense(skel, k * DENSE, x)
        delta = [jnp.maximum(a - b, 0.0) for a, b in zip(v, d)]
        if delta_ref is not None:
            store_dense(delta_ref, k * DENSE, x, delta)
        s = [a + jnp.maximum(b - a * b, 0.0) for a, b in zip(s, delta)]
        store_dense(skel, (k + 1) * DENSE, x, s)
        return 0

    lax.fori_loop(first, last, row, 0)


def forward_kernel(
    pred, target, rows_a, rows_b, cols_a, cols_b, vol, skel, delta, cot, skel_target, sums, tvol, tskel
):
    unpack(pred, target, rows_a, rows_b, cols_a, cols_b, vol, tvol)
    skel[0:DENSE, :] = jnp.zeros((DENSE, 128), jnp.float32)
    tskel[0:DENSE, :] = jnp.zeros((DENSE, 128), jnp.float32)
    five, four = Axes(5), Axes(4)
    near = WIDE - NEAR
    end = WIDE + OWN + NEAR

    def step(k, _):
        erode_rows(vol, k, 1 + k, 35 - k, five)
        erode_rows(tvol, k, near + 1 + k, end - 1 - k, four)
        skeleton_rows(vol, k, near, end, four, skel, delta)
        skeleton_rows(tvol, k, WIDE, WIDE + OWN, four, tskel, None)
        return 0

    lax.fori_loop(0, ITERS + 1, step, 0)
    sub = sublanes()
    own_y = (sub >= 2) & (sub < 6)
    inside_y = jnp.logical_not(((sub < 2) & four.first_y) | ((sub >= 6) & four.last_y))
    done = (ITERS + 1) * DENSE
    zero = jnp.zeros((8, 128), jnp.float32)

    def total(x, acc):
        sp, st = load_dense(skel, done, x), load_dense(tskel, done, x)
        p, t = load(vol, 0, x, 4), load(tvol, 0, x, 4)
        a = acc[0] + sum(u * w for u, w in zip(sp, t))
        c = acc[2] + sum(u * w for u, w in zip(st, p))
        store_dense(skel_target, 0, x - WIDE, st)
        return a, acc[1] + sum(sp), c, acc[3] + sum(st)

    acc = lax.fori_loop(WIDE, WIDE + OWN, total, (zero,) * 4)
    lane = lax.broadcasted_iota(jnp.int32, (8, 128), 1)
    row = jnp.zeros((8, 128), jnp.float32)
    for i in range(4):
        row = jnp.where(lane == i, jnp.sum(jnp.where(own_y, acc[i], 0.0)), row)
    for i in range(sums.shape[0] // 8):
        sums[i * 8 : i * 8 + 8, :] = row

    def start(x, _):
        outside = ((x < WIDE) & four.first_x) | ((x >= WIDE + OWN) & four.last_x)
        keep = inside_y & jnp.logical_not(outside)
        t = load(tvol, 0, x, 4)
        store_dense(cot, 0, x, [jnp.where(keep, a, 0.0) for a in t])
        store_dense(cot, DENSE, x, [jnp.where(keep, 1.0, 0.0)] * 4)
        return 0

    lax.fori_loop(near, end, start, 0)


def split_weight(v, other, tie):
    return jnp.where(v > other, 0.0, jnp.where(v == other, tie, 1.0))


def split_weight_min(v, other, tie):
    return jnp.where(v < other, 0.0, jnp.where(v == other, tie, 1.0))


def pool_weights(v, low, up, q, minimum):
    pick, weight = (jnp.minimum, split_weight_min) if minimum else (jnp.maximum, split_weight)
    t = pick(low, v)
    to_up = weight(t, up, 0.5)
    to_low = weight(v, low, q)
    return to_low * (1.0 - to_up), to_up, pick(t, up)


def backward_kernel(vol, skel, delta, cot, grad_t, grad_1, gs, ga, gd):
    axes = Axes(4)
    near, end = WIDE - NEAR, WIDE + OWN + NEAR
    gs[...] = cot[...]
    ga[...] = jnp.zeros((2 * DENSE, 128), jnp.float32)
    zeros = [jnp.zeros((8, 128), jnp.float32)] * 4
    pair = (0, DENSE)

    def step(i, _):
        k = ITERS - i
        base = k * PLANE

        def undilate(x, carry):
            below, above = axes.rows(x, LOW)
            e = load(vol, base + PLANE, x, 4)
            low_x, up_x = load(vol, base + PLANE, below, 4), load(vol, base + PLANE, above, 4)
            q_x = axes.q_x(x)
            d, s = load_dense(delta, k * DENSE, x), load_dense(skel, k * DENSE, x)
            wx = [pool_weights(a, b, c, q_x, False) for a, b, c in zip(e, low_x, up_x)]
            a = [w[2] for w in wx]
            low, up = axes.along_y(a, -INF)
            wy = [pool_weights(a[j], low[j], up[j], axes.q_y if j == axes.up_b else 0.5, False) for j in range(4)]
            b = [w[2] for w in wy]
            low, up = axes.along_z(b, -INF)
            wz = [pool_weights(b[j], low[j], up[j], axes.q_z, False) for j in range(4)]
            out = []
            for c, at in enumerate(pair):
                pending, ahead = carry[c]
                g = load_dense(gs, at, x)
                kept = [jnp.where(u - v * u > 0.0, w, 0.0) for u, v, w in zip(d, s, g)]
                store_dense(gs, at, x, [w - m * u for u, m, w in zip(d, kept, g)])
                g = [jnp.where(u > 0.0, m * (1.0 - v), 0.0) for u, v, m in zip(d, s, kept)]
                store_dense(gd, at, x, g)
                gl, gu = [h * w[0] for h, w in zip(g, wz)], [h * w[1] for h, w in zip(g, wz)]
                g = [h - m - n + o for h, m, n, o in zip(g, gl, gu, back_z(gl, gu))]
                gl, gu = [h * w[0] for h, w in zip(g, wy)], [h * w[1] for h, w in zip(g, wy)]
                g = [h - m - n + o for h, m, n, o in zip(g, gl, gu, axes.back_y(gl, gu))]
                gl, gu = [h * w[0] for h, w in zip(g, wx)], [h * w[1] for h, w in zip(g, wx)]
                g = [h - m - n + o for h, m, n, o in zip(g, gl, gu, ahead)]
                old = load_dense(ga, at, x - 1)
                store_dense(ga, at, x - 1, [h - m - n for h, m, n in zip(old, pending, gl)])
                out.append((g, gu))
            return out

        lax.fori_loop(8 - k, 28 + k, undilate, [(zeros, zeros)] * 2)

        def unerode(x, carry):
            below, above = axes.rows(x, HIGH)
            v = load(vol, base, x, 4)
            low_x, up_x = load(vol, base, below, 4), load(vol, base, above, 4)
            q_x = axes.q_x(x)
            wx = [pool_weights(a, b, c, q_x, True) for a, b, c in zip(v, low_x, up_x)]
            low, up = axes.along_y(v, INF)
            wy = [pool_weights(v[j], low[j], up[j], axes.q_y if j == axes.up_b else 0.5, True) for j in range(4)]
            low, up = axes.along_z(v, INF)
            wz = [pool_weights(v[j], low[j], up[j], axes.q_z, True) for j in range(4)]
            share = []
            for j in range(4):
                one, two, three = wx[j][2], wy[j][2], wz[j][2]
                to_three = split_weight_min(jnp.minimum(one, two), three, 0.5)
                rest = 1.0 - to_three
                to_two = split_weight_min(one, two, 0.5) * rest
                to_one = rest - to_two
                share.append(
                    (to_one * wx[j][0], to_one * wx[j][1], to_two * wy[j][0], to_two * wy[j][1],
                     to_three * wz[j][0], to_three * wz[j][1])
                )
            out = []
            for c, at in enumerate(pair):
                pending, ahead = carry[c]
                g = load_dense(ga, at, x)
                parts = [[h * w[n] for h, w in zip(g, share)] for n in range(6)]
                for part in parts:
                    g = [h - m for h, m in zip(g, part)]
                g = each(jnp.add, g, axes.back_y(parts[2], parts[3]), back_z(parts[4], parts[5]), ahead)
                direct = load_dense(gd, at, x - 1)
                store_dense(ga, at, x - 1, each(jnp.add, direct, pending, parts[0]))
                out.append((g, parts[1]))
            return out

        lax.fori_loop(9 - k, 27 + k, unerode, [(zeros, zeros)] * 2)
        return 0

    lax.fori_loop(0, ITERS + 1, step, 0)
    own = pl.ds(WIDE * LV, OWN * LV)
    grad_t[...] = ga[own, :]
    grad_1[...] = ga[pl.ds(DENSE + WIDE * LV, OWN * LV), :]


def finish_kernel(cells, sums, grad_t, grad_1, skel_target, gradient, loss, natural):
    total = jnp.zeros((8, 128), jnp.float32)
    for i in range(sums.shape[0] // 8):
        total = total + sums[i * 8 : i * 8 + 8, :]
    lane = lanes()
    sum_a, sum_b, sum_c, sum_d = (
        jnp.broadcast_to(jnp.sum(jnp.where(lane == i, total, 0.0)), (8, 128)) for i in range(4)
    )
    precision = (sum_a + 1.0) / (sum_b + 1.0)
    sensitivity = (sum_c + 1.0) / (sum_d + 1.0)
    together = precision + sensitivity
    loss[...] = 1.0 - 2.0 * precision * sensitivity / together
    coef_pred = cells * (-2.0 * sensitivity * sensitivity / (together * together)) / (sum_b + 1.0)
    coef_target = cells * (-2.0 * precision * precision / (together * together)) / (sum_d + 1.0)

    def row(x, _):
        t, one, s = load_dense(grad_t, 0, x), load_dense(grad_1, 0, x), load_dense(skel_target, 0, x)
        for b in range(4):
            natural[pl.ds(x * LV + b, 8, stride=4), :] = (
                coef_pred * (t[b] - precision * one[b]) + coef_target * s[b]
            )
        return 0

    lax.fori_loop(0, OWN, row, 0)
    for x in range(OWN):
        gradient[x * OWN : (x + 1) * OWN, :] = natural[x * LV + 8 : x * LV + 24, :]


def call(kernel, out, scratch=(), cost=None):
    vmem = pl.BlockSpec(memory_space=pltpu.VMEM)

    def run(*args):
        return pl.pallas_call(
            kernel,
            out_shape=[jax.ShapeDtypeStruct(s, jnp.float32) for s in out],
            in_specs=[vmem] * len(args),
            out_specs=[vmem] * len(out),
            scratch_shapes=[pltpu.VMEM(s, jnp.float32) for s in scratch],
            compiler_params=pltpu.CompilerParams(vmem_limit_bytes=12 * 2**20),
            cost_estimate=cost,
        )(*args)

    return run


def swapped(value, axis, shift):
    size = lax.axis_size(axis)
    pairs = [((i + shift) % size, ((i ^ 1) + shift) % size) for i in range(size)]
    return lax.ppermute(value, axis, pairs)


def body(prediction, label_mask, confidence):
    rows, cols, planes = prediction.shape
    flat = (rows * cols, planes)
    devices = lax.axis_size("gx") * lax.axis_size("gy")
    cells = float(devices * rows * cols * planes)
    pred = prediction.reshape(flat)
    side = ((WIDE + NEAR) * OWN, 128)
    target, send_a, send_b = call(pack_rows_kernel, [flat, side, side])(
        pred, label_mask.reshape(flat), confidence.reshape(flat)
    )
    rows_a, rows_b = swapped(send_a, "gx", 0), swapped(send_b, "gx", 1)
    side = (SEND, 128)
    send_a, send_b = call(
        pack_columns_kernel, [side, side], [(XB * 8 * OWN, 128), (TB * 8 * OWN, 128)]
    )(pred, target, rows_a, rows_b)
    cols_a, cols_b = swapped(send_a, "gy", 0), swapped(send_b, "gy", 1)
    levels = ITERS + 2
    vol, skel, delta, cot, skel_target, sums = call(
        forward_kernel,
        [(levels * PLANE, 128), (levels * DENSE, 128), ((ITERS + 1) * DENSE, 128), (2 * DENSE, 128), (OWN * LV, 128), (devices, 128)],
        [(levels * PLANE, 128), (levels * DENSE, 128)],
    )(pred, target, rows_a, rows_b, cols_a, cols_b)
    sums = lax.all_to_all(sums.reshape(devices, 1, 128), ("gx", "gy"), 0, 0).reshape(devices, 128)
    grad_t, grad_1 = call(
        backward_kernel,
        [(OWN * LV, 128)] * 2,
        [(2 * DENSE, 128)] * 3,
        pl.CostEstimate(flops=100_000_000, bytes_accessed=20_000_000, transcendentals=0),
    )(vol, skel, delta, cot)

    def finish(*refs):
        finish_kernel(jnp.float32(cells), *refs)

    gradient, loss = call(finish, [flat, (8, 128)], [(OWN * LV, 128)])(sums, grad_t, grad_1, skel_target)
    return gradient.reshape(rows, cols, planes), loss[0, 0]


def solution(mesh):
    placed = (P("gx", "gy", None), P("gx", "gy", None), P("gx", "gy", None))
    return jax.shard_map(
        body, mesh=mesh, in_specs=placed, out_specs=(P("gx", "gy", None), P()), check_vma=False
    )
```

profile of v0, /device:TPU:1, one launch (start us, length us, event | category | flops | bytes accessed | tf_op | source)
XLA Modules:
  0.0 118.0 jit_solution(350232136718758561)
XLA Ops:
  0.6 0.0 copy-start.6
  0.6 0.9 copy-done.6
  1.5 0.9 copy-done.13
  2.4 0.9 copy-done.14
  3.4 2.6 %collective-permute-start = (f32[240,128]{1,0:T(8,128)S(1)}, f32[240,128]{1,0:T(8,128)S(1)}, u32[]{:S(2)}, u32[]{:S(2)}) collective-permute-start(f32[240,128]{1,0:T(8,128)S(1)} %get-tuple-element.18), channel_id=1, source_target_pairs={{0,16},{16,0},{32,48},{48,32},{64,80},{80,64},{96,112},{112,96},{1... | collective-permute-start | bytes 368648 | tf_op jit(solution)/shard_map/ppermute | solution.py:434
  5.9 7.1 %collective-permute-start.1 = (f32[240,128]{1,0:T(8,128)S(1)}, f32[240,128]{1,0:T(8,128)S(1)}, u32[]{:S(2)}, u32[]{:S(2)}) collective-permute-start(f32[240,128]{1,0:T(8,128)S(1)} %get-tuple-element.19), channel_id=1, source_target_pairs={{16,32},{32,16},{48,64},{64,48},{80,96},{96,80},{112,128},{128,112... | collective-permute-start | bytes 368648 | tf_op jit(solution)/shard_map/ppermute | solution.py:434
  13.1 0.0 collective-permute-done.rows_a
  13.1 2.7 %collective-permute-done.1.rows_b = f32[240,128]{1,0:T(8,128)S(1)} collective-permute-done((f32[240,128]{1,0:T(8,128)S(1)}, f32[240,128]{1,0:T(8,128)S(1)}, u32[]{:S(2)}, u32[]{:S(2)}) %collective-permute-start.1) | collective-permute-done | bytes 122912 | tf_op jit(solution)/shard_map/ppermute | solution.py:434
  15.8 0.2 shard_map.51
  16.0 1.6 %collective-permute-start.2 = (f32[560,128]{1,0:T(8,128)S(1)}, f32[560,128]{1,0:T(8,128)S(1)}, u32[]{:S(2)}, u32[]{:S(2)}) collective-permute-start(f32[560,128]{1,0:T(8,128)S(1)} %get-tuple-element.20), channel_id=1, source_target_pairs={{0,1},{1,0},{2,3},{3,2},{4,5},{5,4},{6,7},{7,6},{8,9},{9,8},{10,11... | collective-permute-start | bytes 860168 | tf_op jit(solution)/shard_map/ppermute | solution.py:434
  17.6 0.3 collective-permute-start.3
  17.9 0.9 collective-permute-done.2.cols_a
  18.8 7.9 %collective-permute-done.3.cols_b = f32[560,128]{1,0:T(8,128)S(1)} collective-permute-done((f32[560,128]{1,0:T(8,128)S(1)}, f32[560,128]{1,0:T(8,128)S(1)}, u32[]{:S(2)}, u32[]{:S(2)}) %collective-permute-start.3) | collective-permute-done | bytes 286752 | tf_op jit(solution)/shard_map/ppermute | solution.py:434
  26.7 32.9 %shard_map.52 = (f32[8000,128]{1,0:T(8,128)S(1)}, f32[6400,128]{1,0:T(8,128)S(1)}, f32[5120,128]{1,0:T(8,128)S(1)}, f32[2560,128]{1,0:T(8,128)S(1)}, f32[512,128]{1,0:T(8,128)S(1)}, /*index=5*/f32[256,128]{1,0:T(8,128)}) custom-call(f32[256,128]{1,0:T(8,128)S(1)} %bitcast.11, f32[256,128]{1,0:T(8,128)S(1)} %get-tuple-element.17.target, ...), custom_call_target="tpu_custom_call" | custom-call | tf_op jit(solution)/shard_map/pallas_call | solution.py:418
  59.6 1.9 %copy-done = f32[8000,128]{1,0:T(8,128)} copy-done((f32[8000,128]{1,0:T(8,128)}, f32[8000,128]{1,0:T(8,128)S(1)}, u32[]{:S(2)}) %copy-start) | copy-done | bytes 4096024
  61.5 1.5 %copy-done.2 = f32[5120,128]{1,0:T(8,128)} copy-done((f32[5120,128]{1,0:T(8,128)}, f32[5120,128]{1,0:T(8,128)S(1)}, u32[]{:S(2)}) %copy-start.2) | copy-done | bytes 2621464
  63.1 1.1 copy-done.4
  64.1 0.7 copy-done.7
  64.9 10.7 %all-to-all-start = ((f32[256,1,128]{2,1,0:T(1,128)}), f32[256,1,128]{2,1,0:T(1,128)S(1)}, u32[]{:S(2)}, u32[]{:S(2)}) async-start(f32[256,1,128]{2,1,0:T(1,128)} %bitcast.4), calls=%async_computation | async-start | bytes 262144 | tf_op jit(solution)/shard_map/all_to_all | solution.py:459
  75.6 0.0 copy-start.1
  75.6 2.2 %copy-done.1 = f32[8000,128]{1,0:T(8,128)S(1)} copy-done((f32[8000,128]{1,0:T(8,128)S(1)}, f32[8000,128]{1,0:T(8,128)}, u32[]{:S(2)}) %copy-start.1) | copy-done | bytes 4096024
  77.7 1.7 %copy-done.3 = f32[5120,128]{1,0:T(8,128)S(1)} copy-done((f32[5120,128]{1,0:T(8,128)S(1)}, f32[5120,128]{1,0:T(8,128)}, u32[]{:S(2)}) %copy-start.3) | copy-done | bytes 2621464
  79.5 1.3 %copy-done.5 = f32[2560,128]{1,0:T(8,128)S(1)} copy-done((f32[2560,128]{1,0:T(8,128)S(1)}, f32[2560,128]{1,0:T(8,128)}, u32[]{:S(2)}) %copy-start.5) | copy-done | bytes 1310744
  80.8 31.5 %shard_map.53 = (f32[512,128]{1,0:T(8,128)S(1)}, f32[512,128]{1,0:T(8,128)S(1)}) custom-call(f32[8000,128]{1,0:T(8,128)S(1)} %copy-done.1, f32[6400,128]{1,0:T(8,128)S(1)} %get-tuple-element.24.skel, f32[5120,128]{1,0:T(8,128)S(1)} %copy-done.3, f32[2560,128]{1,0:T(8,128)S(1)} %copy-done.5), custom_call_target="tpu_custom_call" | custom-call | flops 100000000 | bytes 20000000 | tf_op jit(solution)/shard_map/pallas_call | solution.py:418
  112.3 0.7 copy-done.9
  113.0 0.7 copy-done.11
  113.7 0.0 all-to-all-done
  113.7 0.9 copy-done.8
  114.6 0.9 copy-done.10
  115.6 0.9 copy-done.12
  116.5 1.0 shard_map.54
  117.5 0.5 slice.3
  (14 shorter events, 0.1 us)
Async XLA Ops:
  0.6 0.9 copy-start.6
  1.5 0.9 copy-start.13
  2.4 0.9 copy-start.14
  3.4 9.7 %collective-permute-start = (f32[240,128]{1,0:T(8,128)S(1)}, f32[240,128]{1,0:T(8,128)S(1)}, u32[]{:S(2)}, u32[]{:S(2)}) collective-permute-start(f32[240,128]{1,0:T(8,128)S(1)} %get-tuple-element.18), channel_id=1, source_target_pairs={{0,16},{16,0},{32,48},{48,32},{64,80},{80,64},{96,112},{112,96},{1... | collective-permute-start | bytes 368648 | tf_op jit(solution)/shard_map/ppermute | solution.py:434
  5.9 9.9 %collective-permute-start.1 = (f32[240,128]{1,0:T(8,128)S(1)}, f32[240,128]{1,0:T(8,128)S(1)}, u32[]{:S(2)}, u32[]{:S(2)}) collective-permute-start(f32[240,128]{1,0:T(8,128)S(1)} %get-tuple-element.19), channel_id=1, source_target_pairs={{16,32},{32,16},{48,64},{64,48},{80,96},{96,80},{112,128},{128,112... | collective-permute-start | bytes 368648 | tf_op jit(solution)/shard_map/ppermute | solution.py:434
  16.0 2.8 %collective-permute-start.2 = (f32[560,128]{1,0:T(8,128)S(1)}, f32[560,128]{1,0:T(8,128)S(1)}, u32[]{:S(2)}, u32[]{:S(2)}) collective-permute-start(f32[560,128]{1,0:T(8,128)S(1)} %get-tuple-element.20), channel_id=1, source_target_pairs={{0,1},{1,0},{2,3},{3,2},{4,5},{5,4},{6,7},{7,6},{8,9},{9,8},{10,11... | collective-permute-start | bytes 860168 | tf_op jit(solution)/shard_map/ppermute | solution.py:434
  17.6 9.1 %collective-permute-start.3 = (f32[560,128]{1,0:T(8,128)S(1)}, f32[560,128]{1,0:T(8,128)S(1)}, u32[]{:S(2)}, u32[]{:S(2)}) collective-permute-start(f32[560,128]{1,0:T(8,128)S(1)} %get-tuple-element.21), channel_id=1, source_target_pairs={{1,2},{2,1},{3,4},{4,3},{5,6},{6,5},{7,8},{8,7},{9,10},{10,9},{11,... | collective-permute-start | bytes 860168 | tf_op jit(solution)/shard_map/ppermute | solution.py:434
  59.6 1.9 %copy-start = (f32[8000,128]{1,0:T(8,128)}, f32[8000,128]{1,0:T(8,128)S(1)}, u32[]{:S(2)}) copy-start(f32[8000,128]{1,0:T(8,128)S(1)} %get-tuple-element.23.vol) | copy-start | bytes 12288004
  61.5 1.5 %copy-start.2 = (f32[5120,128]{1,0:T(8,128)}, f32[5120,128]{1,0:T(8,128)S(1)}, u32[]{:S(2)}) copy-start(f32[5120,128]{1,0:T(8,128)S(1)} %get-tuple-element.25.delta) | copy-start | bytes 7864324
  63.1 1.1 copy-start.4
  64.1 0.7 copy-start.7
  64.9 48.8 %all-to-all-start = ((f32[256,1,128]{2,1,0:T(1,128)}), f32[256,1,128]{2,1,0:T(1,128)S(1)}, u32[]{:S(2)}, u32[]{:S(2)}) async-start(f32[256,1,128]{2,1,0:T(1,128)} %bitcast.4), calls=%async_computation | async-start | bytes 262144 | tf_op jit(solution)/shard_map/all_to_all | solution.py:459
  75.6 2.2 %copy-start.1 = (f32[8000,128]{1,0:T(8,128)S(1)}, f32[8000,128]{1,0:T(8,128)}, u32[]{:S(2)}) copy-start(f32[8000,128]{1,0:T(8,128)} %copy-done) | copy-start | bytes 12288004
  77.7 1.7 %copy-start.3 = (f32[5120,128]{1,0:T(8,128)S(1)}, f32[5120,128]{1,0:T(8,128)}, u32[]{:S(2)}) copy-start(f32[5120,128]{1,0:T(8,128)} %copy-done.2) | copy-start | bytes 7864324
  79.5 1.3 %copy-start.5 = (f32[2560,128]{1,0:T(8,128)S(1)}, f32[2560,128]{1,0:T(8,128)}, u32[]{:S(2)}) copy-start(f32[2560,128]{1,0:T(8,128)} %copy-done.4) | copy-start | bytes 3932164
  112.3 0.7 copy-start.9
  113.0 0.7 copy-start.11
  113.7 1.0 copy-start.8
  114.6 0.9 copy-start.10
  115.6 0.9 copy-start.12
where the time goes:
time: 118 us
  Pallas kernels  65.6 us (56%)
  starting transfers between devices  22.3 us (19%)
  local copies, waits for them, and re-layouts  17.9 us (15%)
  waiting for transfers between devices  11.5 us (10%)
    pallas_call x5, Pallas kernels, run(): pl.pallas_call(kernel, out_shape=[jax.ShapeDtypeStruct(s, jnp.float32) fo...  65.6 us
    unnamed x30, local copies, waits for them, and re-layouts  17.4 us
    ppermute x4, starting transfers between devices, swapped(): return lax.ppermute(value, axis, pairs)  11.6 us
    ppermute x4, waiting for transfers between devices, swapped(): return lax.ppermute(value, axis, pairs)  11.5 us
    all_to_all x1, starting transfers between devices, body(): lax.all_to_all(sums.reshape(devices, 1, 128), ('gx', 'gy'), 0, 0)  10.7 us
  transfers between devices with their start and end apart: 5, of which 3 were waited for; matrix products, arithmetic and copies ran while one was open for 0% of the time, Pallas kernels for 27%

commit v1 on v0

--- a/solution.py
+++ b/solution.py
@@ -6,17 +6,17 @@
 from jax.sharding import PartitionSpec as P
 
 ITERS = 3
+RE, RD, RU, RV = 4, 4, 4, 4
 OWN = 16
 WIDE = 10
 NEAR = 5
 YP = 40
 Y0 = 12
 XP = 40
-HIGH, LOW = 36, 37
+HIGH, LOW = 2.0, -1.0
 PLANE = XP * YP
 LV = 32
 DENSE = XP * LV
-INF = float("inf")
 
 
 def lanes():
@@ -44,10 +44,12 @@
         self.q_y = jnp.where(self.up_y, 0.25, 0.5)
         self.q_z = jnp.where(self.up_z, 0.25, 0.5)
 
-    def rows(self, x, stand_in):
-        below = jnp.where((x == WIDE) & self.first_x, stand_in, x - 1)
-        above = jnp.where((x == WIDE + OWN - 1) & self.last_x, stand_in, x + 1)
-        return below, above
+    def fence(self, ref, base, value):
+        for face, x in ((self.first_x, WIDE - 1), (self.last_x, WIDE + OWN)):
+
+            @pl.when(face)
+            def _(x=x):
+                ref[pl.ds(pl.multiple_of(base + x * YP, 8), YP), :] = jnp.full((YP, 128), value, jnp.float32)
 
     def q_x(self, x):
         return jnp.where((x == WIDE + OWN - 1) & self.last_x, 0.25, 0.5)
@@ -181,50 +183,51 @@
                 tvol[pl.ds((NEAR + i * 8) * YP + y + j, 8, stride=YP), :] = ref[
                     pl.ds((WIDE * XB + j * TB + i) * 8, 8), :
                 ]
-    for ref in (vol, tvol):
-        for k in range(ITERS + 2):
-            ref[pl.ds(k * PLANE + HIGH * YP, YP), :] = jnp.full((YP, 128), INF, jnp.float32)
-            ref[pl.ds(k * PLANE + LOW * YP, YP), :] = jnp.full((YP, 128), -INF, jnp.float32)
-
-
-def erode_rows(vol, k, first, last, axes):
+
+
+def erode_rows(vol, k, first, count, axes):
     nb = axes.nb
     base = k * PLANE
-
-    def row(x, _):
-        below, above = axes.rows(x, HIGH)
-        v = load(vol, base, x, nb)
-        low, up = load(vol, base, below, nb), load(vol, base, above, nb)
-        m = each(jnp.minimum, v, low, up, *axes.along_y(v, INF), *axes.along_z(v, INF))
-        store(vol, base + PLANE, x, nb, m)
-        return 0
-
-    lax.fori_loop(first, last, row, 0)
-
-
-def dilated(vol, base, x, axes):
-    below, above = axes.rows(x, LOW)
-    e = load(vol, base, x, 4)
-    a = each(jnp.maximum, e, load(vol, base, below, 4), load(vol, base, above, 4))
-    b = each(jnp.maximum, a, *axes.along_y(a, -INF))
-    return each(jnp.maximum, b, *axes.along_z(b, -INF))
-
-
-def skeleton_rows(vol, k, first, last, axes, skel, delta_ref):
+    axes.fence(vol, base, HIGH)
+
+    def group(i, _):
+        x = first + i * RE
+        v = [load(vol, base, x + j - 1, nb) for j in range(RE + 2)]
+        m = [
+            each(jnp.minimum, v[j], v[j - 1], v[j + 1], *axes.along_y(v[j], HIGH), *axes.along_z(v[j], HIGH))
+            for j in range(1, RE + 1)
+        ]
+        for j in range(RE):
+            store(vol, base + PLANE, x + j, nb, m[j])
+        return 0
+
+    lax.fori_loop(0, lax.div(count + RE - 1, RE), group, 0)
+
+
+def skeleton_rows(vol, k, first, count, axes, skel, delta_ref):
     base = k * PLANE
-
-    def row(x, _):
-        d = dilated(vol, base + PLANE, x, axes)
-        v = load(vol, base, x, 4)
-        s = load_dense(skel, k * DENSE, x)
-        delta = [jnp.maximum(a - b, 0.0) for a, b in zip(v, d)]
-        if delta_ref is not None:
-            store_dense(delta_ref, k * DENSE, x, delta)
-        s = [a + jnp.maximum(b - a * b, 0.0) for a, b in zip(s, delta)]
-        store_dense(skel, (k + 1) * DENSE, x, s)
-        return 0
-
-    lax.fori_loop(first, last, row, 0)
+    axes.fence(vol, base + PLANE, LOW)
+
+    def group(i, _):
+        x = first + i * RD
+        e = [load(vol, base + PLANE, x + j - 1, 4) for j in range(RD + 2)]
+        v = [load(vol, base, x + j, 4) for j in range(RD)]
+        s = [load_dense(skel, k * DENSE, x + j) for j in range(RD)]
+        deltas, sums = [], []
+        for j in range(RD):
+            a = each(jnp.maximum, e[j + 1], e[j], e[j + 2])
+            b = each(jnp.maximum, a, *axes.along_y(a, LOW))
+            d = each(jnp.maximum, b, *axes.along_z(b, LOW))
+            delta = [jnp.maximum(p - q, 0.0) for p, q in zip(v[j], d)]
+            deltas.append(delta)
+            sums.append([p + jnp.maximum(q - p * q, 0.0) for p, q in zip(s[j], delta)])
+        for j in range(RD):
+            if delta_ref is not None:
+                store_dense(delta_ref, k * DENSE, x + j, deltas[j])
+            store_dense(skel, (k + 1) * DENSE, x + j, sums[j])
+        return 0
+
+    lax.fori_loop(0, (count + RD - 1) // RD, group, 0)
 
 
 def forward_kernel(
@@ -238,10 +241,10 @@
     end = WIDE + OWN + NEAR
 
     def step(k, _):
-        erode_rows(vol, k, 1 + k, 35 - k, five)
-        erode_rows(tvol, k, near + 1 + k, end - 1 - k, four)
-        skeleton_rows(vol, k, near, end, four, skel, delta)
-        skeleton_rows(tvol, k, WIDE, WIDE + OWN, four, tskel, None)
+        erode_rows(vol, k, 1 + k, 34 - 2 * k, five)
+        erode_rows(tvol, k, near + 1 + k, 24 - 2 * k, four)
+        skeleton_rows(vol, k, near, end - near, four, skel, delta)
+        skeleton_rows(tvol, k, WIDE, OWN, four, tskel, None)
         return 0
 
     lax.fori_loop(0, ITERS + 1, step, 0)
@@ -306,75 +309,100 @@
         k = ITERS - i
         base = k * PLANE
 
-        def undilate(x, carry):
-            below, above = axes.rows(x, LOW)
-            e = load(vol, base + PLANE, x, 4)
-            low_x, up_x = load(vol, base + PLANE, below, 4), load(vol, base + PLANE, above, 4)
-            q_x = axes.q_x(x)
-            d, s = load_dense(delta, k * DENSE, x), load_dense(skel, k * DENSE, x)
-            wx = [pool_weights(a, b, c, q_x, False) for a, b, c in zip(e, low_x, up_x)]
-            a = [w[2] for w in wx]
-            low, up = axes.along_y(a, -INF)
-            wy = [pool_weights(a[j], low[j], up[j], axes.q_y if j == axes.up_b else 0.5, False) for j in range(4)]
-            b = [w[2] for w in wy]
-            low, up = axes.along_z(b, -INF)
-            wz = [pool_weights(b[j], low[j], up[j], axes.q_z, False) for j in range(4)]
-            out = []
+        first = 8 - k
+
+        def undilate(i, carry):
+            x = first + i * RU
+            rows = range(RU)
+            e = [load(vol, base + PLANE, x + j - 1, 4) for j in range(RU + 2)]
+            d = [load_dense(delta, k * DENSE, x + j) for j in rows]
+            s = [load_dense(skel, k * DENSE, x + j) for j in rows]
+            g_in = [[load_dense(gs, at, x + j) for j in rows] for at in pair]
+            old = [[load_dense(ga, at, x + j - 1) for j in rows] for at in pair]
+            wx = [
+                [pool_weights(p, q, r, axes.q_x(x + j), False) for p, q, r in zip(e[j + 1], e[j], e[j + 2])] for j in rows
+            ]
+            wy, wz = [], []
+            for j in rows:
+                a = [w[2] for w in wx[j]]
+                low, up = axes.along_y(a, LOW)
+                wy.append(
+                    [pool_weights(a[n], low[n], up[n], axes.q_y if n == axes.up_b else 0.5, False) for n in range(4)]
+                )
+                a = [w[2] for w in wy[j]]
+                low, up = axes.along_z(a, LOW)
+                wz.append([pool_weights(a[n], low[n], up[n], axes.q_z, False) for n in range(4)])
+            out, writes = [], []
             for c, at in enumerate(pair):
                 pending, ahead = carry[c]
-                g = load_dense(gs, at, x)
-                kept = [jnp.where(u - v * u > 0.0, w, 0.0) for u, v, w in zip(d, s, g)]
-                store_dense(gs, at, x, [w - m * u for u, m, w in zip(d, kept, g)])
-                g = [jnp.where(u > 0.0, m * (1.0 - v), 0.0) for u, v, m in zip(d, s, kept)]
-                store_dense(gd, at, x, g)
-                gl, gu = [h * w[0] for h, w in zip(g, wz)], [h * w[1] for h, w in zip(g, wz)]
-                g = [h - m - n + o for h, m, n, o in zip(g, gl, gu, back_z(gl, gu))]
-                gl, gu = [h * w[0] for h, w in zip(g, wy)], [h * w[1] for h, w in zip(g, wy)]
-                g = [h - m - n + o for h, m, n, o in zip(g, gl, gu, axes.back_y(gl, gu))]
-                gl, gu = [h * w[0] for h, w in zip(g, wx)], [h * w[1] for h, w in zip(g, wx)]
-                g = [h - m - n + o for h, m, n, o in zip(g, gl, gu, ahead)]
-                old = load_dense(ga, at, x - 1)
-                store_dense(ga, at, x - 1, [h - m - n for h, m, n in zip(old, pending, gl)])
-                out.append((g, gu))
+                for j in rows:
+                    g = g_in[c][j]
+                    kept = [jnp.where(u - v * u > 0.0, w, 0.0) for u, v, w in zip(d[j], s[j], g)]
+                    writes.append((gs, at, x + j, [w - m * u for u, m, w in zip(d[j], kept, g)]))
+                    g = [jnp.where(u > 0.0, m * (1.0 - v), 0.0) for u, v, m in zip(d[j], s[j], kept)]
+                    writes.append((gd, at, x + j, g))
+                    for w3, back in ((wz[j], back_z), (wy[j], axes.back_y), (wx[j], None)):
+                        gl, gu = [h * w[0] for h, w in zip(g, w3)], [h * w[1] for h, w in zip(g, w3)]
+                        g = [h - m - n for h, m, n in zip(g, gl, gu)]
+                        if back is not None:
+                            g = each(jnp.add, g, back(gl, gu))
+                    writes.append((ga, at, x + j - 1, [h - m - n for h, m, n in zip(old[c][j], pending, gl)]))
+                    pending, ahead = each(jnp.add, g, ahead), gu
+                out.append((pending, ahead))
+            for ref, at, row, v in writes:
+                store_dense(ref, at, row, v)
             return out
 
-        lax.fori_loop(8 - k, 28 + k, undilate, [(zeros, zeros)] * 2)
-
-        def unerode(x, carry):
-            below, above = axes.rows(x, HIGH)
-            v = load(vol, base, x, 4)
-            low_x, up_x = load(vol, base, below, 4), load(vol, base, above, 4)
-            q_x = axes.q_x(x)
-            wx = [pool_weights(a, b, c, q_x, True) for a, b, c in zip(v, low_x, up_x)]
-            low, up = axes.along_y(v, INF)
-            wy = [pool_weights(v[j], low[j], up[j], axes.q_y if j == axes.up_b else 0.5, True) for j in range(4)]
-            low, up = axes.along_z(v, INF)
-            wz = [pool_weights(v[j], low[j], up[j], axes.q_z, True) for j in range(4)]
-            share = []
-            for j in range(4):
-                one, two, three = wx[j][2], wy[j][2], wz[j][2]
-                to_three = split_weight_min(jnp.minimum(one, two), three, 0.5)
-                rest = 1.0 - to_three
-                to_two = split_weight_min(one, two, 0.5) * rest
-                to_one = rest - to_two
-                share.append(
-                    (to_one * wx[j][0], to_one * wx[j][1], to_two * wy[j][0], to_two * wy[j][1],
-                     to_three * wz[j][0], to_three * wz[j][1])
-                )
-            out = []
+        axes.fence(vol, base + PLANE, LOW)
+        lax.fori_loop(0, lax.div(20 + 2 * k + RU - 1, RU), undilate, [(zeros, zeros)] * 2)
+        start = 9 - k
+
+        def unerode(i, carry):
+            x = start + i * RV
+            rows = range(RV)
+            v = [load(vol, base, x + j - 1, 4) for j in range(RV + 2)]
+            g_in = [[load_dense(ga, at, x + j) for j in rows] for at in pair]
+            direct = [[load_dense(gd, at, x + j - 1) for j in rows] for at in pair]
+            shares = []
+            for j in rows:
+                wx = [pool_weights(p, q, r, axes.q_x(x + j), True) for p, q, r in zip(v[j + 1], v[j], v[j + 2])]
+                low, up = axes.along_y(v[j + 1], HIGH)
+                wy = [
+                    pool_weights(v[j + 1][n], low[n], up[n], axes.q_y if n == axes.up_b else 0.5, True)
+                    for n in range(4)
+                ]
+                low, up = axes.along_z(v[j + 1], HIGH)
+                wz = [pool_weights(v[j + 1][n], low[n], up[n], axes.q_z, True) for n in range(4)]
+                share = []
+                for n in range(4):
+                    one, two, three = wx[n][2], wy[n][2], wz[n][2]
+                    to_three = split_weight_min(jnp.minimum(one, two), three, 0.5)
+                    rest = 1.0 - to_three
+                    to_two = split_weight_min(one, two, 0.5) * rest
+                    to_one = rest - to_two
+                    share.append(
+                        (to_one * wx[n][0], to_one * wx[n][1], to_two * wy[n][0], to_two * wy[n][1],
+                         to_three * wz[n][0], to_three * wz[n][1])
+                    )
+                shares.append(share)
+            out, writes = [], []
             for c, at in enumerate(pair):
                 pending, ahead = carry[c]
-                g = load_dense(ga, at, x)
-                parts = [[h * w[n] for h, w in zip(g, share)] for n in range(6)]
-                for part in parts:
-                    g = [h - m for h, m in zip(g, part)]
-                g = each(jnp.add, g, axes.back_y(parts[2], parts[3]), back_z(parts[4], parts[5]), ahead)
-                direct = load_dense(gd, at, x - 1)
-                store_dense(ga, at, x - 1, each(jnp.add, direct, pending, parts[0]))
-                out.append((g, parts[1]))
+                for j in rows:
+                    g = g_in[c][j]
+                    parts = [[h * w[n] for h, w in zip(g, shares[j])] for n in range(6)]
+                    for part in parts:
+                        g = [h - m for h, m in zip(g, part)]
+                    g = each(jnp.add, g, axes.back_y(parts[2], parts[3]), back_z(parts[4], parts[5]), ahead)
+                    writes.append((ga, at, x + j - 1, each(jnp.add, direct[c][j], pending, parts[0])))
+                    pending, ahead = g, parts[1]
+                out.append((pending, ahead))
+            for ref, at, row, v in writes:
+                store_dense(ref, at, row, v)
             return out
 
-        lax.fori_loop(9 - k, 27 + k, unerode, [(zeros, zeros)] * 2)
+        axes.fence(vol, base, HIGH)
+        lax.fori_loop(0, lax.div(18 + 2 * k + RV - 1, RV), unerode, [(zeros, zeros)] * 2)
         return 0
 
     lax.fori_loop(0, ITERS + 1, step, 0)

time: 118 us -> 78.9 us (0.67)
  Pallas kernels: 65.6 us -> 26.2 us
    pallas_call x5, Pallas kernels: 65.6 us -> 26.2 us  [run(): pl.pallas_call(kernel, out_shape=[jax.ShapeDtypeStruct(s, jnp.float32) fo...]
  transfers between devices with their start and end apart: 5 -> 5, of which waited for: 3 -> 3; matrix products, arithmetic and copies ran while one was open for 0% -> 0% of each run, Pallas kernels for 27% -> 16%
where the time goes in v1:
time: 78.9 us; the launch traced here: 78.6 us
  Pallas kernels  26.2 us (33%)
  starting transfers between devices  22.3 us (28%)
  local copies, waits for them, and re-layouts  17.9 us (23%)
  waiting for transfers between devices  11.5 us (15%)
    pallas_call x5, Pallas kernels, run(): pl.pallas_call(kernel, out_shape=[jax.ShapeDtypeStruct(s, jnp.float32) fo...  26.2 us
    unnamed x30, local copies, waits for them, and re-layouts  17.4 us
    ppermute x4, starting transfers between devices, swapped(): return lax.ppermute(value, axis, pairs)  11.6 us
    ppermute x4, waiting for transfers between devices, swapped(): return lax.ppermute(value, axis, pairs)  11.5 us
    all_to_all x1, starting transfers between devices, body(): lax.all_to_all(sums.reshape(devices, 1, 128), ('gx', 'gy'), 0, 0)  10.7 us
  transfers between devices with their start and end apart: 5, of which 3 were waited for; matrix products, arithmetic and copies ran while one was open for 0% of the time, Pallas kernels for 16%

profile of v1, /device:TPU:1, one launch (start us, length us, event | category | flops | bytes accessed | tf_op | source)
XLA Modules:
  0.0 78.6 jit_solution(7078587690463357126)
XLA Ops:
  0.6 0.0 copy-start.6
  0.6 0.9 %copy-done.6 = f32[16,16,128]{2,1,0:T(8,128)S(1)} copy-done((f32[16,16,128]{2,1,0:T(8,128)S(1)}, f32[16,16,128]{2,1,0:T(8,128)}, u32[]{:S(2)}) %copy-start.6) | copy-done | bytes 131096
  1.5 0.9 %copy-done.13 = s32[16,16,128]{2,1,0:T(8,128)S(1)} copy-done((s32[16,16,128]{2,1,0:T(8,128)S(1)}, s32[16,16,128]{2,1,0:T(8,128)}, u32[]{:S(2)}) %copy-start.13) | copy-done | bytes 131096
  2.4 0.9 %copy-done.14 = f32[16,16,128]{2,1,0:T(8,128)S(1)} copy-done((f32[16,16,128]{2,1,0:T(8,128)S(1)}, f32[16,16,128]{2,1,0:T(8,128)}, u32[]{:S(2)}) %copy-start.14) | copy-done | bytes 131096
  3.4 2.6 %collective-permute-start = (f32[240,128]{1,0:T(8,128)S(1)}, f32[240,128]{1,0:T(8,128)S(1)}, u32[]{:S(2)}, u32[]{:S(2)}) collective-permute-start(f32[240,128]{1,0:T(8,128)S(1)} %get-tuple-element.18), channel_id=1, source_target_pairs={{0,16},{16,0},{32,48},{48,32},{64,80},{80,64},{96,112},{112,96},{1... | collective-permute-start | bytes 368648 | tf_op jit(solution)/shard_map/ppermute | solution.py:462
  5.9 7.1 %collective-permute-start.1 = (f32[240,128]{1,0:T(8,128)S(1)}, f32[240,128]{1,0:T(8,128)S(1)}, u32[]{:S(2)}, u32[]{:S(2)}) collective-permute-start(f32[240,128]{1,0:T(8,128)S(1)} %get-tuple-element.19), channel_id=1, source_target_pairs={{16,32},{32,16},{48,64},{64,48},{80,96},{96,80},{112,128},{128,112... | collective-permute-start | bytes 368648 | tf_op jit(solution)/shard_map/ppermute | solution.py:462
  13.1 0.0 collective-permute-done.rows_a
  13.1 2.7 %collective-permute-done.1.rows_b = f32[240,128]{1,0:T(8,128)S(1)} collective-permute-done((f32[240,128]{1,0:T(8,128)S(1)}, f32[240,128]{1,0:T(8,128)S(1)}, u32[]{:S(2)}, u32[]{:S(2)}) %collective-permute-start.1) | collective-permute-done | bytes 122912 | tf_op jit(solution)/shard_map/ppermute | solution.py:462
  15.8 0.2 shard_map.51
  16.0 1.6 %collective-permute-start.2 = (f32[560,128]{1,0:T(8,128)S(1)}, f32[560,128]{1,0:T(8,128)S(1)}, u32[]{:S(2)}, u32[]{:S(2)}) collective-permute-start(f32[560,128]{1,0:T(8,128)S(1)} %get-tuple-element.20), channel_id=1, source_target_pairs={{0,1},{1,0},{2,3},{3,2},{4,5},{5,4},{6,7},{7,6},{8,9},{9,8},{10,11... | collective-permute-start | bytes 860168 | tf_op jit(solution)/shard_map/ppermute | solution.py:462
  17.6 0.3 collective-permute-start.3
  17.9 0.9 %collective-permute-done.2.cols_a = f32[560,128]{1,0:T(8,128)S(1)} collective-permute-done((f32[560,128]{1,0:T(8,128)S(1)}, f32[560,128]{1,0:T(8,128)S(1)}, u32[]{:S(2)}, u32[]{:S(2)}) %collective-permute-start.2) | collective-permute-done | bytes 286752 | tf_op jit(solution)/shard_map/ppermute | solution.py:462
  18.8 7.9 %collective-permute-done.3.cols_b = f32[560,128]{1,0:T(8,128)S(1)} collective-permute-done((f32[560,128]{1,0:T(8,128)S(1)}, f32[560,128]{1,0:T(8,128)S(1)}, u32[]{:S(2)}, u32[]{:S(2)}) %collective-permute-start.3) | collective-permute-done | bytes 286752 | tf_op jit(solution)/shard_map/ppermute | solution.py:462
  26.7 12.6 %shard_map.52 = (f32[8000,128]{1,0:T(8,128)S(1)}, f32[6400,128]{1,0:T(8,128)S(1)}, f32[5120,128]{1,0:T(8,128)S(1)}, f32[2560,128]{1,0:T(8,128)S(1)}, f32[512,128]{1,0:T(8,128)S(1)}, /*index=5*/f32[256,128]{1,0:T(8,128)}) custom-call(f32[256,128]{1,0:T(8,128)S(1)} %bitcast.11, f32[256,128]{1,0:T(8,128)S(1)} %get-tuple-element.17.target, ...), custom_call_target="tpu_custom_call" | custom-call | tf_op jit(solution)/shard_map/pallas_call | solution.py:446
  39.3 1.9 %copy-done = f32[8000,128]{1,0:T(8,128)} copy-done((f32[8000,128]{1,0:T(8,128)}, f32[8000,128]{1,0:T(8,128)S(1)}, u32[]{:S(2)}) %copy-start) | copy-done | bytes 4096024
  41.3 1.5 %copy-done.2 = f32[5120,128]{1,0:T(8,128)} copy-done((f32[5120,128]{1,0:T(8,128)}, f32[5120,128]{1,0:T(8,128)S(1)}, u32[]{:S(2)}) %copy-start.2) | copy-done | bytes 2621464
  42.8 1.1 %copy-done.4 = f32[2560,128]{1,0:T(8,128)} copy-done((f32[2560,128]{1,0:T(8,128)}, f32[2560,128]{1,0:T(8,128)S(1)}, u32[]{:S(2)}) %copy-start.4) | copy-done | bytes 1310744
  43.9 0.7 copy-done.7
  44.6 10.7 %all-to-all-start = ((f32[256,1,128]{2,1,0:T(1,128)}), f32[256,1,128]{2,1,0:T(1,128)S(1)}, u32[]{:S(2)}, u32[]{:S(2)}) async-start(f32[256,1,128]{2,1,0:T(1,128)} %bitcast.4), calls=%async_computation | async-start | bytes 262144 | tf_op jit(solution)/shard_map/all_to_all | solution.py:487
  55.3 2.2 %copy-done.1 = f32[8000,128]{1,0:T(8,128)S(1)} copy-done((f32[8000,128]{1,0:T(8,128)S(1)}, f32[8000,128]{1,0:T(8,128)}, u32[]{:S(2)}) %copy-start.1) | copy-done | bytes 4096024
  57.4 1.7 %copy-done.3 = f32[5120,128]{1,0:T(8,128)S(1)} copy-done((f32[5120,128]{1,0:T(8,128)S(1)}, f32[5120,128]{1,0:T(8,128)}, u32[]{:S(2)}) %copy-start.3) | copy-done | bytes 2621464
  59.2 1.3 %copy-done.5 = f32[2560,128]{1,0:T(8,128)S(1)} copy-done((f32[2560,128]{1,0:T(8,128)S(1)}, f32[2560,128]{1,0:T(8,128)}, u32[]{:S(2)}) %copy-start.5) | copy-done | bytes 1310744
  60.5 12.3 %shard_map.53 = (f32[512,128]{1,0:T(8,128)S(1)}, f32[512,128]{1,0:T(8,128)S(1)}) custom-call(f32[8000,128]{1,0:T(8,128)S(1)} %copy-done.1, f32[6400,128]{1,0:T(8,128)S(1)} %get-tuple-element.24.skel, f32[5120,128]{1,0:T(8,128)S(1)} %copy-done.3, f32[2560,128]{1,0:T(8,128)S(1)} %copy-done.5), custom_call_target="tpu_custom_call" | custom-call | flops 100000000 | bytes 20000000 | tf_op jit(solution)/shard_map/pallas_call | solution.py:446
  72.8 0.0 copy-start.9
  72.8 0.7 copy-done.9
  73.5 0.7 copy-done.11
  74.2 0.0 all-to-all-done
  74.2 0.9 %copy-done.8 = f32[512,128]{1,0:T(8,128)S(1)} copy-done((f32[512,128]{1,0:T(8,128)S(1)}, f32[512,128]{1,0:T(8,128)}, u32[]{:S(2)}) %copy-start.8) | copy-done | bytes 262168
  75.2 0.9 %copy-done.10 = f32[512,128]{1,0:T(8,128)S(1)} copy-done((f32[512,128]{1,0:T(8,128)S(1)}, f32[512,128]{1,0:T(8,128)}, u32[]{:S(2)}) %copy-start.10) | copy-done | bytes 262168
  76.1 0.9 %copy-done.12 = f32[512,128]{1,0:T(8,128)S(1)} copy-done((f32[512,128]{1,0:T(8,128)S(1)}, f32[512,128]{1,0:T(8,128)}, u32[]{:S(2)}) %copy-start.12) | copy-done | bytes 262168
  77.1 1.0 %shard_map.54 = (f32[256,128]{1,0:T(8,128)}, f32[8,128]{1,0:T(8,128)S(1)}) custom-call(f32[256,128]{1,0:T(8,128)S(1)} %bitcast.12, f32[512,128]{1,0:T(8,128)S(1)} %copy-done.10, f32[512,128]{1,0:T(8,128)S(1)} %copy-done.12, f32[512,128]{1,0:T(8,128)S(1)} %copy-done.8), custom_call_target="tpu_custom_call" | custom-call | tf_op jit(solution)/shard_map/pallas_call | solution.py:446
  78.1 0.5 slice.3
  (14 shorter events, 0.1 us)
Async XLA Ops:
  0.6 0.9 %copy-start.6 = (f32[16,16,128]{2,1,0:T(8,128)S(1)}, f32[16,16,128]{2,1,0:T(8,128)}, u32[]{:S(2)}) copy-start(f32[16,16,128]{2,1,0:T(8,128)} %param.3) | copy-start | bytes 393220
  1.5 0.9 %copy-start.13 = (s32[16,16,128]{2,1,0:T(8,128)S(1)}, s32[16,16,128]{2,1,0:T(8,128)}, u32[]{:S(2)}) copy-start(s32[16,16,128]{2,1,0:T(8,128)} %param.4) | copy-start | bytes 393220
  2.4 0.9 %copy-start.14 = (f32[16,16,128]{2,1,0:T(8,128)S(1)}, f32[16,16,128]{2,1,0:T(8,128)}, u32[]{:S(2)}) copy-start(f32[16,16,128]{2,1,0:T(8,128)} %param.5) | copy-start | bytes 393220
  3.4 9.7 %collective-permute-start = (f32[240,128]{1,0:T(8,128)S(1)}, f32[240,128]{1,0:T(8,128)S(1)}, u32[]{:S(2)}, u32[]{:S(2)}) collective-permute-start(f32[240,128]{1,0:T(8,128)S(1)} %get-tuple-element.18), channel_id=1, source_target_pairs={{0,16},{16,0},{32,48},{48,32},{64,80},{80,64},{96,112},{112,96},{1... | collective-permute-start | bytes 368648 | tf_op jit(solution)/shard_map/ppermute | solution.py:462
  5.9 9.9 %collective-permute-start.1 = (f32[240,128]{1,0:T(8,128)S(1)}, f32[240,128]{1,0:T(8,128)S(1)}, u32[]{:S(2)}, u32[]{:S(2)}) collective-permute-start(f32[240,128]{1,0:T(8,128)S(1)} %get-tuple-element.19), channel_id=1, source_target_pairs={{16,32},{32,16},{48,64},{64,48},{80,96},{96,80},{112,128},{128,112... | collective-permute-start | bytes 368648 | tf_op jit(solution)/shard_map/ppermute | solution.py:462
  16.0 2.8 %collective-permute-start.2 = (f32[560,128]{1,0:T(8,128)S(1)}, f32[560,128]{1,0:T(8,128)S(1)}, u32[]{:S(2)}, u32[]{:S(2)}) collective-permute-start(f32[560,128]{1,0:T(8,128)S(1)} %get-tuple-element.20), channel_id=1, source_target_pairs={{0,1},{1,0},{2,3},{3,2},{4,5},{5,4},{6,7},{7,6},{8,9},{9,8},{10,11... | collective-permute-start | bytes 860168 | tf_op jit(solution)/shard_map/ppermute | solution.py:462
  17.6 9.1 %collective-permute-start.3 = (f32[560,128]{1,0:T(8,128)S(1)}, f32[560,128]{1,0:T(8,128)S(1)}, u32[]{:S(2)}, u32[]{:S(2)}) collective-permute-start(f32[560,128]{1,0:T(8,128)S(1)} %get-tuple-element.21), channel_id=1, source_target_pairs={{1,2},{2,1},{3,4},{4,3},{5,6},{6,5},{7,8},{8,7},{9,10},{10,9},{11,... | collective-permute-start | bytes 860168 | tf_op jit(solution)/shard_map/ppermute | solution.py:462
  39.3 1.9 %copy-start = (f32[8000,128]{1,0:T(8,128)}, f32[8000,128]{1,0:T(8,128)S(1)}, u32[]{:S(2)}) copy-start(f32[8000,128]{1,0:T(8,128)S(1)} %get-tuple-element.23.vol) | copy-start | bytes 12288004
  41.3 1.5 %copy-start.2 = (f32[5120,128]{1,0:T(8,128)}, f32[5120,128]{1,0:T(8,128)S(1)}, u32[]{:S(2)}) copy-start(f32[5120,128]{1,0:T(8,128)S(1)} %get-tuple-element.25.delta) | copy-start | bytes 7864324
  42.8 1.1 %copy-start.4 = (f32[2560,128]{1,0:T(8,128)}, f32[2560,128]{1,0:T(8,128)S(1)}, u32[]{:S(2)}) copy-start(f32[2560,128]{1,0:T(8,128)S(1)} %get-tuple-element.26.cot) | copy-start | bytes 3932164
  43.9 0.7 copy-start.7
  44.6 29.7 %all-to-all-start = ((f32[256,1,128]{2,1,0:T(1,128)}), f32[256,1,128]{2,1,0:T(1,128)S(1)}, u32[]{:S(2)}, u32[]{:S(2)}) async-start(f32[256,1,128]{2,1,0:T(1,128)} %bitcast.4), calls=%async_computation | async-start | bytes 262144 | tf_op jit(solution)/shard_map/all_to_all | solution.py:487
  55.3 2.2 %copy-start.1 = (f32[8000,128]{1,0:T(8,128)S(1)}, f32[8000,128]{1,0:T(8,128)}, u32[]{:S(2)}) copy-start(f32[8000,128]{1,0:T(8,128)} %copy-done) | copy-start | bytes 12288004
  57.4 1.7 %copy-start.3 = (f32[5120,128]{1,0:T(8,128)S(1)}, f32[5120,128]{1,0:T(8,128)}, u32[]{:S(2)}) copy-start(f32[5120,128]{1,0:T(8,128)} %copy-done.2) | copy-start | bytes 7864324
  59.2 1.3 %copy-start.5 = (f32[2560,128]{1,0:T(8,128)S(1)}, f32[2560,128]{1,0:T(8,128)}, u32[]{:S(2)}) copy-start(f32[2560,128]{1,0:T(8,128)} %copy-done.4) | copy-start | bytes 3932164
  72.8 0.7 copy-start.9
  73.5 0.7 copy-start.11
  74.2 1.0 %copy-start.8 = (f32[512,128]{1,0:T(8,128)S(1)}, f32[512,128]{1,0:T(8,128)}, u32[]{:S(2)}) copy-start(f32[512,128]{1,0:T(8,128)} %copy-done.7) | copy-start | bytes 786436
  75.2 0.9 %copy-start.10 = (f32[512,128]{1,0:T(8,128)S(1)}, f32[512,128]{1,0:T(8,128)}, u32[]{:S(2)}) copy-start(f32[512,128]{1,0:T(8,128)} %copy-done.9) | copy-start | bytes 786436
  76.1 0.9 %copy-start.12 = (f32[512,128]{1,0:T(8,128)S(1)}, f32[512,128]{1,0:T(8,128)}, u32[]{:S(2)}) copy-start(f32[512,128]{1,0:T(8,128)} %copy-done.11) | copy-start | bytes 786436

commit v2 on v1

--- a/solution.py
+++ b/solution.py
@@ -6,7 +6,7 @@
 from jax.sharding import PartitionSpec as P
 
 ITERS = 3
-RE, RD, RU, RV = 4, 4, 4, 4
+RE, RD, RT, RU, RV = 9, 7, 8, 5, 6
 OWN = 16
 WIDE = 10
 NEAR = 5
@@ -98,6 +98,15 @@
         ref[pl.ds(pl.multiple_of(base + x * LV + 8 * b, 8), 8), :] = v[b]
 
 
+def inside_columns(axes):
+    sub = sublanes()
+    return jnp.logical_not(((sub < 2) & axes.first_y) | ((sub >= 6) & axes.last_y))
+
+
+def inside_row(x, axes):
+    return jnp.logical_not(((x < WIDE) & axes.first_x) | ((x >= WIDE + OWN) & axes.last_x))
+
+
 def each(pick, *lists):
     out = lists[0]
     for other in lists[1:]:
@@ -105,7 +114,15 @@
     return out
 
 
-def pack_rows_kernel(pred, label, conf, target, send_a, send_b):
+def pack_rows_kernel(pred_in, label_in, conf_in, pred, target, send_a, send_b, label, conf, sems):
+    copies = [
+        pltpu.make_async_copy(src, dst, sems.at[i])
+        for i, (src, dst) in enumerate(((pred_in, pred), (label_in, label), (conf_in, conf)))
+    ]
+    for copy in copies:
+        copy.start()
+    for copy in copies:
+        copy.wait()
     even = lax.rem(lax.axis_index("gx"), 2) == 0
     target[...] = label[...].astype(jnp.float32) * conf[...]
     wide, near = WIDE * OWN, NEAR * OWN
@@ -204,34 +221,66 @@
     lax.fori_loop(0, lax.div(count + RE - 1, RE), group, 0)
 
 
-def skeleton_rows(vol, k, first, count, axes, skel, delta_ref):
+def skeleton_rows(vol, k, first, count, axes, skel, delta_ref, take):
     base = k * PLANE
     axes.fence(vol, base + PLANE, LOW)
 
     def group(i, _):
-        x = first + i * RD
-        e = [load(vol, base + PLANE, x + j - 1, 4) for j in range(RD + 2)]
-        v = [load(vol, base, x + j, 4) for j in range(RD)]
-        s = [load_dense(skel, k * DENSE, x + j) for j in range(RD)]
+        x = first + i * take
+        e = [load(vol, base + PLANE, x + j - 1, 4) for j in range(take + 2)]
+        v = [load(vol, base, x + j, 4) for j in range(take)]
+        s = [load_dense(skel, k * DENSE, x + j) for j in range(take)]
         deltas, sums = [], []
-        for j in range(RD):
+        for j in range(take):
             a = each(jnp.maximum, e[j + 1], e[j], e[j + 2])
             b = each(jnp.maximum, a, *axes.along_y(a, LOW))
             d = each(jnp.maximum, b, *axes.along_z(b, LOW))
             delta = [jnp.maximum(p - q, 0.0) for p, q in zip(v[j], d)]
             deltas.append(delta)
             sums.append([p + jnp.maximum(q - p * q, 0.0) for p, q in zip(s[j], delta)])
-        for j in range(RD):
+        for j in range(take):
             if delta_ref is not None:
                 store_dense(delta_ref, k * DENSE, x + j, deltas[j])
             store_dense(skel, (k + 1) * DENSE, x + j, sums[j])
         return 0
 
-    lax.fori_loop(0, (count + RD - 1) // RD, group, 0)
+    lax.fori_loop(0, (count + take - 1) // take, group, 0)
+
+
+KEPT, SAVED = 30, 28
+FROM, START = 4, WIDE - NEAR
+
+
+def kept(ref, at, plane=0, packed=False):
+    if packed:
+        return ref.at[pl.ds(plane * KEPT * YP, KEPT * YP), :]
+    return ref.at[pl.ds(at + FROM * YP, KEPT * YP), :]
+
+
+def saved(ref, at, plane=0, packed=False):
+    if packed:
+        return ref.at[pl.ds(plane * SAVED * LV, SAVED * LV), :]
+    return ref.at[pl.ds(at + START * LV, SAVED * LV), :]
+
+
+def state(vol, skel, delta, cot, far):
+    vol_h, skel_h, delta_h, cot_h = far
+    levels = ITERS + 1
+    pairs = [(saved(cot, 0), saved(cot_h, 0, 0, True)), (kept(vol, levels * PLANE), kept(vol_h, 0, levels, True))]
+    for k in range(ITERS, -1, -1):
+        pairs.append((saved(delta, k * DENSE), saved(delta_h, 0, k, True)))
+        pairs.append((kept(vol, k * PLANE), kept(vol_h, 0, k, True)))
+        if k:
+            pairs.append((saved(skel, k * DENSE), saved(skel_h, 0, k - 1, True)))
+    return pairs
+
+
+COPIES = 2 + 3 * (ITERS + 1) - 1
 
 
 def forward_kernel(
-    pred, target, rows_a, rows_b, cols_a, cols_b, vol, skel, delta, cot, skel_target, sums, tvol, tskel
+    pred, target, rows_a, rows_b, cols_a, cols_b, vol_h, skel_h, delta_h, cot_h, skel_target, sums,
+    vol, skel, delta, cot, tvol, tskel, sems,
 ):
     unpack(pred, target, rows_a, rows_b, cols_a, cols_b, vol, tvol)
     skel[0:DENSE, :] = jnp.zeros((DENSE, 128), jnp.float32)
@@ -239,19 +288,41 @@
     five, four = Axes(5), Axes(4)
     near = WIDE - NEAR
     end = WIDE + OWN + NEAR
+    masks = inside_columns(four)
+
+    def start(x, _):
+        keep = masks & inside_row(x, four)
+        store_dense(cot, 0, x, [jnp.where(keep, a, 0.0) for a in load(tvol, 0, x, 4)])
+        return 0
+
+    lax.fori_loop(near, end, start, 0)
 
     def step(k, _):
         erode_rows(vol, k, 1 + k, 34 - 2 * k, five)
+        skeleton_rows(vol, k, near, end - near, four, skel, delta, RD)
+        return 0
+
+    lax.fori_loop(0, ITERS + 1, step, 0)
+    copies = [
+        pltpu.make_async_copy(src, dst, sems.at[i])
+        for i, (src, dst) in enumerate(state(vol, skel, delta, cot, (vol_h, skel_h, delta_h, cot_h)))
+    ]
+    for copy in copies:
+        copy.start()
+
+    def step(k, _):
         erode_rows(tvol, k, near + 1 + k, 24 - 2 * k, four)
-        skeleton_rows(vol, k, near, end - near, four, skel, delta)
-        skeleton_rows(tvol, k, WIDE, OWN, four, tskel, None)
+        skeleton_rows(tvol, k, WIDE, OWN, four, tskel, None, RT)
         return 0
 
     lax.fori_loop(0, ITERS + 1, step, 0)
+    done = (ITERS + 1) * DENSE
+    copies.append(
+        pltpu.make_async_copy(tskel.at[pl.ds(done + WIDE * LV, OWN * LV), :], skel_target, sems.at[COPIES])
+    )
+    copies[-1].start()
     sub = sublanes()
     own_y = (sub >= 2) & (sub < 6)
-    inside_y = jnp.logical_not(((sub < 2) & four.first_y) | ((sub >= 6) & four.last_y))
-    done = (ITERS + 1) * DENSE
     zero = jnp.zeros((8, 128), jnp.float32)
 
     def total(x, acc):
@@ -259,7 +330,6 @@
         p, t = load(vol, 0, x, 4), load(tvol, 0, x, 4)
         a = acc[0] + sum(u * w for u, w in zip(sp, t))
         c = acc[2] + sum(u * w for u, w in zip(st, p))
-        store_dense(skel_target, 0, x - WIDE, st)
         return a, acc[1] + sum(sp), c, acc[3] + sum(st)
 
     acc = lax.fori_loop(WIDE, WIDE + OWN, total, (zero,) * 4)
@@ -270,15 +340,8 @@
     for i in range(sums.shape[0] // 8):
         sums[i * 8 : i * 8 + 8, :] = row
 
-    def start(x, _):
-        outside = ((x < WIDE) & four.first_x) | ((x >= WIDE + OWN) & four.last_x)
-        keep = inside_y & jnp.logical_not(outside)
-        t = load(tvol, 0, x, 4)
-        store_dense(cot, 0, x, [jnp.where(keep, a, 0.0) for a in t])
-        store_dense(cot, DENSE, x, [jnp.where(keep, 1.0, 0.0)] * 4)
-        return 0
-
-    lax.fori_loop(near, end, start, 0)
+    for copy in copies:
+        copy.wait()
 
 
 def split_weight(v, other, tie):
@@ -297,13 +360,28 @@
     return to_low * (1.0 - to_up), to_up, pick(t, up)
 
 
-def backward_kernel(vol, skel, delta, cot, grad_t, grad_1, gs, ga, gd):
+def backward_kernel(vol_h, skel_h, delta_h, cot_h, grad_t, grad_1, vol, skel, delta, gs, ga, gd, sems):
+    copies = [
+        pltpu.make_async_copy(src, dst, sems.at[i])
+        for i, (dst, src) in enumerate(state(vol, skel, delta, gs, (vol_h, skel_h, delta_h, cot_h)))
+    ]
+    for copy in copies:
+        copy.start()
     axes = Axes(4)
     near, end = WIDE - NEAR, WIDE + OWN + NEAR
-    gs[...] = cot[...]
     ga[...] = jnp.zeros((2 * DENSE, 128), jnp.float32)
+    skel[0:DENSE, :] = jnp.zeros((DENSE, 128), jnp.float32)
+    masks = inside_columns(axes)
+
+    def ones(x, _):
+        store_dense(gs, DENSE, x, [jnp.where(masks & inside_row(x, axes), 1.0, 0.0)] * 4)
+        return 0
+
+    lax.fori_loop(near, end + 2, ones, 0)
     zeros = [jnp.zeros((8, 128), jnp.float32)] * 4
     pair = (0, DENSE)
+    for copy in copies:
+        copy.wait()
 
     def step(i, _):
         k = ITERS - i
@@ -406,12 +484,23 @@
         return 0
 
     lax.fori_loop(0, ITERS + 1, step, 0)
-    own = pl.ds(WIDE * LV, OWN * LV)
-    grad_t[...] = ga[own, :]
-    grad_1[...] = ga[pl.ds(DENSE + WIDE * LV, OWN * LV), :]
-
-
-def finish_kernel(cells, sums, grad_t, grad_1, skel_target, gradient, loss, natural):
+    copies = [
+        pltpu.make_async_copy(ga.at[pl.ds(at + WIDE * LV, OWN * LV), :], out, sems.at[i])
+        for i, (at, out) in enumerate(((0, grad_t), (DENSE, grad_1)))
+    ]
+    for copy in copies:
+        copy.start()
+    for copy in copies:
+        copy.wait()
+
+
+def finish_kernel(cells, sums, far_t, far_1, far_skel, gradient, loss, natural, grad_t, grad_1, skel_target, sems):
+    copies = [
+        pltpu.make_async_copy(src, dst, sems.at[i])
+        for i, (src, dst) in enumerate(((far_t, grad_t), (far_1, grad_1), (far_skel, skel_target)))
+    ]
+    for copy in copies:
+        copy.start()
     total = jnp.zeros((8, 128), jnp.float32)
     for i in range(sums.shape[0] // 8):
         total = total + sums[i * 8 : i * 8 + 8, :]
@@ -422,9 +511,11 @@
     precision = (sum_a + 1.0) / (sum_b + 1.0)
     sensitivity = (sum_c + 1.0) / (sum_d + 1.0)
     together = precision + sensitivity
-    loss[...] = 1.0 - 2.0 * precision * sensitivity / together
+    loss[...] = (1.0 - 2.0 * precision * sensitivity / together)[0:1, 0:1]
     coef_pred = cells * (-2.0 * sensitivity * sensitivity / (together * together)) / (sum_b + 1.0)
     coef_target = cells * (-2.0 * precision * precision / (together * together)) / (sum_d + 1.0)
+    for copy in copies:
+        copy.wait()
 
     def row(x, _):
         t, one, s = load_dense(grad_t, 0, x), load_dense(grad_1, 0, x), load_dense(skel_target, 0, x)
@@ -439,17 +530,23 @@
         gradient[x * OWN : (x + 1) * OWN, :] = natural[x * LV + 8 : x * LV + 24, :]
 
 
-def call(kernel, out, scratch=(), cost=None):
-    vmem = pl.BlockSpec(memory_space=pltpu.VMEM)
+def call(kernel, out, scratch=(), cost=None, copies=0, far_in=(), far_out=()):
+    near, far = pl.BlockSpec(memory_space=pltpu.VMEM), pl.BlockSpec(memory_space=pltpu.HBM)
+    scratch = [pltpu.VMEM(s, d) for s, d in ((s, jnp.float32) if isinstance(s[0], int) else s for s in scratch)]
+    if copies:
+        scratch.append(pltpu.SemaphoreType.DMA((copies,)))
 
     def run(*args):
+        args = [pltpu.with_memory_space_constraint(a, pltpu.HBM) if i in far_in else a for i, a in enumerate(args)]
         return pl.pallas_call(
             kernel,
-            out_shape=[jax.ShapeDtypeStruct(s, jnp.float32) for s in out],
-            in_specs=[vmem] * len(args),
-            out_specs=[vmem] * len(out),
-            scratch_shapes=[pltpu.VMEM(s, jnp.float32) for s in scratch],
-            compiler_params=pltpu.CompilerParams(vmem_limit_bytes=12 * 2**20),
+            out_shape=[
+                (pltpu.HBM if i in far_out else jax.ShapeDtypeStruct)(s, jnp.float32) for i, s in enumerate(out)
+            ],
+            in_specs=[far if i in far_in else near for i in range(len(args))],
+            out_specs=[far if i in far_out else near for i in range(len(out))],
+            scratch_shapes=scratch,
+            compiler_params=pltpu.CompilerParams(vmem_limit_bytes=32 * 2**20),
             cost_estimate=cost,
         )(*args)
 
@@ -467,11 +564,10 @@
     flat = (rows * cols, planes)
     devices = lax.axis_size("gx") * lax.axis_size("gy")
     cells = float(devices * rows * cols * planes)
-    pred = prediction.reshape(flat)
     side = ((WIDE + NEAR) * OWN, 128)
-    target, send_a, send_b = call(pack_rows_kernel, [flat, side, side])(
-        pred, label_mask.reshape(flat), confidence.reshape(flat)
-    )
+    pred, target, send_a, send_b = call(
+        pack_rows_kernel, [flat, flat, side, side], [(flat, jnp.int32), flat], copies=3, far_in=(0, 1, 2)
+    )(prediction.reshape(flat), label_mask.reshape(flat), confidence.reshape(flat))
     rows_a, rows_b = swapped(send_a, "gx", 0), swapped(send_b, "gx", 1)
     side = (SEND, 128)
     send_a, send_b = call(
@@ -479,24 +575,36 @@
     )(pred, target, rows_a, rows_b)
     cols_a, cols_b = swapped(send_a, "gy", 0), swapped(send_b, "gy", 1)
     levels = ITERS + 2
-    vol, skel, delta, cot, skel_target, sums = call(
+    own, saved_rows = (OWN * LV, 128), SAVED * LV
+    vols, dense = (levels * PLANE, 128), (levels * DENSE, 128)
+    *far, skel_target, sums = call(
         forward_kernel,
-        [(levels * PLANE, 128), (levels * DENSE, 128), ((ITERS + 1) * DENSE, 128), (2 * DENSE, 128), (OWN * LV, 128), (devices, 128)],
-        [(levels * PLANE, 128), (levels * DENSE, 128)],
+        [
+            (levels * KEPT * YP, 128), (ITERS * saved_rows, 128), ((ITERS + 1) * saved_rows, 128), (saved_rows, 128),
+            own, (devices, 128),
+        ],
+        [vols, dense, dense, (DENSE, 128), vols, dense],
+        copies=COPIES + 1,
+        far_out=(0, 1, 2, 3, 4),
     )(pred, target, rows_a, rows_b, cols_a, cols_b)
     sums = lax.all_to_all(sums.reshape(devices, 1, 128), ("gx", "gy"), 0, 0).reshape(devices, 128)
     grad_t, grad_1 = call(
         backward_kernel,
-        [(OWN * LV, 128)] * 2,
-        [(2 * DENSE, 128)] * 3,
+        [own, own],
+        [vols, dense, dense] + [(2 * DENSE, 128)] * 3,
         pl.CostEstimate(flops=100_000_000, bytes_accessed=20_000_000, transcendentals=0),
-    )(vol, skel, delta, cot)
+        copies=COPIES,
+        far_in=(0, 1, 2, 3),
+        far_out=(0, 1),
+    )(*far)
 
     def finish(*refs):
         finish_kernel(jnp.float32(cells), *refs)
 
-    gradient, loss = call(finish, [flat, (8, 128)], [(OWN * LV, 128)])(sums, grad_t, grad_1, skel_target)
-    return gradient.reshape(rows, cols, planes), loss[0, 0]
+    gradient, loss = call(finish, [flat, (1, 1)], [own] * 4, copies=3, far_in=(1, 2, 3))(
+        sums, grad_t, grad_1, skel_target
+    )
+    return gradient.reshape(rows, cols, planes), loss.reshape(())
 
 
 def solution(mesh):

time: 78.9 us -> 63.1 us (0.80)
  local copies, waits for them, and re-layouts: 17.9 us -> 0 us
  Pallas kernels: 26.2 us -> 28.5 us
    unnamed x30 -> x0, local copies, waits for them, and re-layouts: 17.4 us -> none
    pallas_call x5, Pallas kernels: 26.2 us -> 28.5 us  [run(): pl.pallas_call(kernel, out_shape=[(pltpu.HBM if i in far_out else jax.Sha...]
  transfers between devices with their start and end apart: 5 -> 5, of which waited for: 3 -> 3; matrix products, arithmetic and copies ran while one was open for 0% -> 0% of each run, Pallas kernels for 16% -> 24%
where the time goes in v2:
time: 63.1 us; the launch traced here: 63 us
  Pallas kernels  28.5 us (45%)
  starting transfers between devices  22.3 us (35%)
  waiting for transfers between devices  11.5 us (18%)
  between operations  0.68 us (1%)
    pallas_call x5, Pallas kernels, run(): pl.pallas_call(kernel, out_shape=[(pltpu.HBM if i in far_out else jax.Sha...  28.5 us
    ppermute x4, starting transfers between devices, swapped(): return lax.ppermute(value, axis, pairs)  11.6 us
    ppermute x4, waiting for transfers between devices, swapped(): return lax.ppermute(value, axis, pairs)  11.5 us
    all_to_all x1, starting transfers between devices, body(): lax.all_to_all(sums.reshape(devices, 1, 128), ('gx', 'gy'), 0, 0)  10.7 us
  transfers between devices with their start and end apart: 5, of which 3 were waited for; matrix products, arithmetic and copies ran while one was open for 0% of the time, Pallas kernels for 24%

profile of v2, /device:TPU:1, one launch (start us, length us, event | category | flops | bytes accessed | tf_op | source)
XLA Modules:
  0.0 63.0 jit_solution(12712904683767965592)
XLA Ops:
  0.6 1.1 %shard_map.50 = (f32[256,128]{1,0:T(8,128)S(1)}, f32[256,128]{1,0:T(8,128)S(1)}, f32[240,128]{1,0:T(8,128)S(1)}, f32[240,128]{1,0:T(8,128)S(1)}) custom-call(f32[256,128]{1,0:T(8,128)} %bitcast.10, s32[256,128]{1,0:T(8,128)} %bitcast.11, f32[256,128]{1,0:T(8,128)} %bitcast.12), custom_call_target="tpu_custom_call" | custom-call | tf_op jit(solution)/shard_map/pallas_call | solution.py:541
  1.7 2.6 %collective-permute-start = (f32[240,128]{1,0:T(8,128)S(1)}, f32[240,128]{1,0:T(8,128)S(1)}, u32[]{:S(2)}, u32[]{:S(2)}) collective-permute-start(f32[240,128]{1,0:T(8,128)S(1)} %get-tuple-element.20), channel_id=1, source_target_pairs={{0,16},{16,0},{32,48},{48,32},{64,80},{80,64},{96,112},{112,96},{1... | collective-permute-start | bytes 368648 | tf_op jit(solution)/shard_map/ppermute | solution.py:559
  4.3 7.1 %collective-permute-start.1 = (f32[240,128]{1,0:T(8,128)S(1)}, f32[240,128]{1,0:T(8,128)S(1)}, u32[]{:S(2)}, u32[]{:S(2)}) collective-permute-start(f32[240,128]{1,0:T(8,128)S(1)} %get-tuple-element.21), channel_id=1, source_target_pairs={{16,32},{32,16},{48,64},{64,48},{80,96},{96,80},{112,128},{128,112... | collective-permute-start | bytes 368648 | tf_op jit(solution)/shard_map/ppermute | solution.py:559
  11.4 0.0 collective-permute-done.rows_a
  11.4 2.7 %collective-permute-done.1.rows_b = f32[240,128]{1,0:T(8,128)S(1)} collective-permute-done((f32[240,128]{1,0:T(8,128)S(1)}, f32[240,128]{1,0:T(8,128)S(1)}, u32[]{:S(2)}, u32[]{:S(2)}) %collective-permute-start.1) | collective-permute-done | bytes 122912 | tf_op jit(solution)/shard_map/ppermute | solution.py:559
  14.1 0.2 shard_map.51
  14.4 1.6 %collective-permute-start.2 = (f32[560,128]{1,0:T(8,128)S(1)}, f32[560,128]{1,0:T(8,128)S(1)}, u32[]{:S(2)}, u32[]{:S(2)}) collective-permute-start(f32[560,128]{1,0:T(8,128)S(1)} %get-tuple-element.22), channel_id=1, source_target_pairs={{0,1},{1,0},{2,3},{3,2},{4,5},{5,4},{6,7},{7,6},{8,9},{9,8},{10,11... | collective-permute-start | bytes 860168 | tf_op jit(solution)/shard_map/ppermute | solution.py:559
  16.0 0.3 collective-permute-start.3
  16.3 0.9 %collective-permute-done.2.cols_a = f32[560,128]{1,0:T(8,128)S(1)} collective-permute-done((f32[560,128]{1,0:T(8,128)S(1)}, f32[560,128]{1,0:T(8,128)S(1)}, u32[]{:S(2)}, u32[]{:S(2)}) %collective-permute-start.2) | collective-permute-done | bytes 286752 | tf_op jit(solution)/shard_map/ppermute | solution.py:559
  17.2 7.9 %collective-permute-done.3.cols_b = f32[560,128]{1,0:T(8,128)S(1)} collective-permute-done((f32[560,128]{1,0:T(8,128)S(1)}, f32[560,128]{1,0:T(8,128)S(1)}, u32[]{:S(2)}, u32[]{:S(2)}) %collective-permute-start.3) | collective-permute-done | bytes 286752 | tf_op jit(solution)/shard_map/ppermute | solution.py:559
  25.1 10.0 %shard_map.52 = (f32[6000,128]{1,0:T(8,128)}, f32[2688,128]{1,0:T(8,128)}, f32[3584,128]{1,0:T(8,128)}, f32[896,128]{1,0:T(8,128)}, f32[512,128]{1,0:T(8,128)}, /*index=5*/f32[256,128]{1,0:T(8,128)}) custom-call(f32[256,128]{1,0:T(8,128)S(1)} %get-tuple-element.18.pred, f32[256,128]{1,0:T(8,128)S(1)} %get-tuple-element.19.target, ...), custom_call_target="tpu_custom_call" | custom-call | tf_op jit(solution)/shard_map/pallas_call | solution.py:541
  35.1 10.7 %all-to-all-start = ((f32[256,1,128]{2,1,0:T(1,128)}), f32[256,1,128]{2,1,0:T(1,128)S(1)}, u32[]{:S(2)}, u32[]{:S(2)}) async-start(f32[256,1,128]{2,1,0:T(1,128)} %bitcast.4), calls=%async_computation | async-start | bytes 262144 | tf_op jit(solution)/shard_map/all_to_all | solution.py:590
  45.8 15.2 %shard_map.53 = (f32[512,128]{1,0:T(8,128)}, f32[512,128]{1,0:T(8,128)}) custom-call(f32[6000,128]{1,0:T(8,128)} %get-tuple-element.25.vol_h, f32[2688,128]{1,0:T(8,128)} %get-tuple-element.26.skel_h, f32[3584,128]{1,0:T(8,128)} %get-tuple-element.27.delta_h, f32[896,128]{1,0:T(8,128)} %get-tuple-element.28.cot_h), custom_call_target="tpu_custom_call" | custom-call | flops 100000000 | bytes 20000000 | tf_op jit(solution)/shard_map/pallas_call | solution.py:541
  61.0 0.0 all-to-all-done
  61.0 1.9 %shard_map.54 = (f32[256,128]{1,0:T(8,128)}, f32[1,1]{1,0:T(1,128)}) custom-call(f32[256,128]{1,0:T(8,128)S(1)} %bitcast.9, f32[512,128]{1,0:T(8,128)} %get-tuple-element.29.refs_1_, f32[512,128]{1,0:T(8,128)} %get-tuple-element.30.refs_2_, f32[512,128]{1,0:T(8,128)} %get-tuple-element.31.refs_3_), custom_call_target="tpu_custom_call" | custom-call | tf_op jit(solution)/shard_map/pallas_call | solution.py:541
Async XLA Ops:
  1.7 9.7 %collective-permute-start = (f32[240,128]{1,0:T(8,128)S(1)}, f32[240,128]{1,0:T(8,128)S(1)}, u32[]{:S(2)}, u32[]{:S(2)}) collective-permute-start(f32[240,128]{1,0:T(8,128)S(1)} %get-tuple-element.20), channel_id=1, source_target_pairs={{0,16},{16,0},{32,48},{48,32},{64,80},{80,64},{96,112},{112,96},{1... | collective-permute-start | bytes 368648 | tf_op jit(solution)/shard_map/ppermute | solution.py:559
  4.3 9.9 %collective-permute-start.1 = (f32[240,128]{1,0:T(8,128)S(1)}, f32[240,128]{1,0:T(8,128)S(1)}, u32[]{:S(2)}, u32[]{:S(2)}) collective-permute-start(f32[240,128]{1,0:T(8,128)S(1)} %get-tuple-element.21), channel_id=1, source_target_pairs={{16,32},{32,16},{48,64},{64,48},{80,96},{96,80},{112,128},{128,112... | collective-permute-start | bytes 368648 | tf_op jit(solution)/shard_map/ppermute | solution.py:559
  14.4 2.8 %collective-permute-start.2 = (f32[560,128]{1,0:T(8,128)S(1)}, f32[560,128]{1,0:T(8,128)S(1)}, u32[]{:S(2)}, u32[]{:S(2)}) collective-permute-start(f32[560,128]{1,0:T(8,128)S(1)} %get-tuple-element.22), channel_id=1, source_target_pairs={{0,1},{1,0},{2,3},{3,2},{4,5},{5,4},{6,7},{7,6},{8,9},{9,8},{10,11... | collective-permute-start | bytes 860168 | tf_op jit(solution)/shard_map/ppermute | solution.py:559
  16.0 9.1 %collective-permute-start.3 = (f32[560,128]{1,0:T(8,128)S(1)}, f32[560,128]{1,0:T(8,128)S(1)}, u32[]{:S(2)}, u32[]{:S(2)}) collective-permute-start(f32[560,128]{1,0:T(8,128)S(1)} %get-tuple-element.23), channel_id=1, source_target_pairs={{1,2},{2,1},{3,4},{4,3},{5,6},{6,5},{7,8},{8,7},{9,10},{10,9},{11,... | collective-permute-start | bytes 860168 | tf_op jit(solution)/shard_map/ppermute | solution.py:559
  35.1 26.0 %all-to-all-start = ((f32[256,1,128]{2,1,0:T(1,128)}), f32[256,1,128]{2,1,0:T(1,128)S(1)}, u32[]{:S(2)}, u32[]{:S(2)}) async-start(f32[256,1,128]{2,1,0:T(1,128)} %bitcast.4), calls=%async_computation | async-start | bytes 262144 | tf_op jit(solution)/shard_map/all_to_all | solution.py:590
